TPU v7x, 512 devices: a whole 4x4x16 slice. The times are simulated.
512 devices in a mesh: rows: 64 (over z, x), sub: 8 (over y, core).
Axes of the slice: x: 4, y: 4, z: 16, core: 2. Of those that a mesh axis runs over, the one named last changes fastest.
Arguments:
- basis: float32 [8, 64, 131072], P(None, None, ('rows', 'sub'))
- stiffness: float32 [12, 8, 8, 131072], P(None, None, None, ('rows', 'sub')), as said below
- col_index: int32 [12, 131072], P(None, ('rows', 'sub')), may hold values from 0 to 319, as said below
- block_count: int32 [131072], P(('rows', 'sub')), may hold values from 6 to 12, as said below
- send_list: int32 [2, 16384], P(None, ('rows', 'sub')), may hold values from 0 to 255, as said below
Outputs:
- basis_next: float32 [8, 64, 131072], P(None, None, ('rows', 'sub'))
- factor: float32 [64, 64], replicated
Inputs may be any that keep to these rules, and one draw needn't show every extreme that they name: col_index[0, b] is block row b's own slab-local index. A value v below 256 is a block row of the same slab; 256 + j is the j-th row of the previous slab's send_list[1]; 288 + j is the j-th row of the next slab's send_list[0]. Slots of the first slab may name 256 to 287 and slots of the last slab may name 288 to 319; those ghosts are zeros. Block row b uses slots 0 to block_count[b] - 1; later slots are ignored. `send_list`: in each slab, row 0 holds 32 distinct block rows below 128; row 1 holds 32 distinct block rows at or above 128. stiffness[0, i, i, b] is at least 2.
All inputs are finite; a program needn't handle non-finite values.
Results may differ from a plain program's by a relative error of at most 0.0003.
Values sent between devices are 32-bit elements; how exact they have to be, the bound alone decides.
A program may use at most 128 MiB of HBM per device.

v0:
```python
import jax
import jax.numpy as jnp
from jax import lax
from jax.sharding import PartitionSpec as P

BLOCK = 8
LOADS = 64
RIM = 128


def padded_2(cells, sides, width):
    for axis, dim in sides:
        count = lax.axis_size(axis)
        ends = count - 1
        head = lax.slice_in_dim(cells, 0, width, axis=dim)
        tail = lax.slice_in_dim(cells, cells.shape[dim] - width, cells.shape[dim], axis=dim)
        cells = jnp.concatenate(
            [
                lax.ppermute(tail, axis, [(i, (i + 1) % count) for i in range(ends)]),
                cells,
                lax.ppermute(head, axis, [((i + 1) % count, i) for i in range(ends)]),
            ],
            axis=dim,
        )
    return cells


def slab_product(extended, columns, counts, values):

    def add_slot(slot_idx, total):
        picked = jnp.take(extended, columns[slot_idx], axis=2)
        live_mask = (slot_idx < counts).astype(total.dtype)
        coefficient = values[slot_idx] * live_mask
        return total + jnp.einsum(
            "ijb,jlb->ilb", coefficient, picked, precision=lax.Precision.HIGHEST
        )

    start = jnp.zeros((extended.shape[0], extended.shape[1], columns.shape[1]), jnp.float32)
    total = lax.fori_loop(0, columns.shape[0], add_slot, start)
    pivots = jnp.diagonal(values[0], axis1=0, axis2=1).T
    return total / pivots[:, None, :]


def cholesky_upper(gram):
    order = gram.shape[0]
    counter = jnp.arange(order, dtype=jnp.int32)

    def column_step(index, state):
        remain, upper = state
        unit = (counter == index).astype(jnp.float32)
        pivot_row = jnp.sum(remain * unit[:, None], axis=0)
        pivot = jnp.sqrt(jnp.sum(pivot_row * unit))
        new_row = pivot_row / pivot * (counter >= index).astype(jnp.float32)
        upper = upper + unit[:, None] * new_row[None, :]
        remain = remain - new_row[:, None] * new_row[None, :]
        return (remain, upper)

    start = (gram, jnp.zeros_like(gram))
    return lax.fori_loop(0, order, column_step, start)[1]


def invert_upper(upper):
    order = upper.shape[0]
    counter = jnp.arange(order, dtype=jnp.int32)

    def row_step(step_idx, inverse):
        index = order - 1 - step_idx
        unit = (counter == index).astype(jnp.float32)
        upper_row = jnp.sum(upper * unit[:, None], axis=0)
        pivot = jnp.sum(upper_row * unit)
        partial_value = jnp.dot(upper_row, inverse, precision=lax.Precision.HIGHEST)
        new_row = (unit - partial_value) / pivot
        return inverse + unit[:, None] * new_row[None, :]

    return lax.fori_loop(0, order, row_step, jnp.zeros_like(upper))


def on_device(basis, stiffness, col_index, block_count, send_list):
    slab_rows = basis.shape[2]
    send_count = send_list.shape[1]
    padded = padded_2(basis, ((("rows", "sub"), 2),), RIM)
    lists_all = padded_2(send_list, ((("rows", "sub"), 1),), send_count)
    from_prev = jnp.maximum(lists_all[1, :send_count] - (slab_rows - RIM), 0)
    from_next = lists_all[0, 2 * send_count :] + RIM + slab_rows
    left_ghost = jnp.take(padded, from_prev, axis=2)
    right_ghost = jnp.take(padded, from_next, axis=2)
    extended = jnp.concatenate([basis, left_ghost, right_ghost], axis=2)
    scaled = slab_product(extended, col_index, block_count, stiffness)
    total_rows = BLOCK * slab_rows * lax.axis_size(("rows", "sub"))
    transposed = jnp.transpose(scaled, (1, 0, 2)).reshape(LOADS, BLOCK * slab_rows)
    local_gram = jnp.dot(transposed, transposed.T, precision=lax.Precision.HIGHEST) / total_rows
    total_gram = lax.psum(local_gram, ("rows", "sub"))
    upper_factor = cholesky_upper(total_gram)
    inverse = invert_upper(upper_factor)
    solved = jnp.dot(inverse.T, transposed, precision=lax.Precision.HIGHEST)
    basis_next = jnp.transpose(solved.reshape(LOADS, BLOCK, slab_rows), (1, 0, 2))
    return (basis_next, upper_factor)


def solution(mesh):
    in_specs = (
        P(None, None, ("rows", "sub")),
        P(None, None, None, ("rows", "sub")),
        P(None, ("rows", "sub")),
        P(("rows", "sub")),
        P(None, ("rows", "sub")),
    )
    out_specs = (P(None, None, ("rows", "sub")), P())
    return jax.shard_map(
        on_device, mesh=mesh, in_specs=in_specs, out_specs=out_specs, check_vma=False
    )
```

profile of v0, /device:TPU:1, one launch (start us, length us, event | category | flops | bytes accessed | tf_op | source)
XLA Modules:
  0.0 448.5 jit_solution(10093552684190539941)
XLA Ops:
  0.6 4.6 %collective-permute-start.2 = (s32[2,32]{1,0:T(2,128)}, s32[2,32]{1,0:T(2,128)S(1)}, u32[]{:S(2)}, u32[]{:S(2)}) collective-permute-start(s32[2,32]{1,0:T(2,128)} %param.17), channel_id=1, source_target_pairs={{0,1},{1,2},{2,3},{3,4},{4,5},{5,6},{6,7},{7,8},{8,9},{9,10},{10,1... | collective-permute-start | bytes 776 | tf_op jit(solution)/shard_map/ppermute | solution.py:19
  5.2 5.5 %collective-permute-start.3 = (s32[2,32]{1,0:T(2,128)}, s32[2,32]{1,0:T(2,128)S(1)}, u32[]{:S(2)}, u32[]{:S(2)}) collective-permute-start(s32[2,32]{1,0:T(2,128)} %param.17), channel_id=1, source_target_pairs={{1,0},{2,1},{3,2},{4,3},{5,4},{6,5},{7,6},{8,7},{9,8},{10,9},{11,1... | collective-permute-start | bytes 776 | tf_op jit(solution)/shard_map/ppermute | solution.py:21
  15.0 3.2 collective-permute-start.1
  21.4 4.2 collective-permute-done.1
  25.6 2.7 pad_maximum_fusion
  28.3 2.2 gather_fusion.2
  30.4 2.2 gather_fusion.3
  33.9 92.9 %while.45 = (s32[]{:T(128)}, f32[8,64,256]{1,0,2:T(8,128)S(1)}, s32[12,256]{1,0:T(8,128)}, f32[8,64,320]{1,0,2:T(8,128)}, f32[12,8,8,256]{3,2,1,0:T(8,128)}, /*index=5*/s32[256]{0:T(256)S(1)}, s32[]{:T(128)}, s32[]{:T(128)}) while((s32[]{:T(128)}, f32[8,64,256]{1,0,2:T(8,128)S(1)}, s32[12,256]{1,0:T(8,128)}, ...), condition=%wide.region_1.3_spmd.clone, body=%wide.region_0.0_spmd.clone.sunk | while | flops 12996355 | bytes 2963051 | solution.py:39
  38.0 3.6 fusion.34
  42.4 2.1 gather_fusion
  45.7 3.6 fusion.34
  50.1 2.1 gather_fusion
  53.5 3.6 fusion.34
  57.9 2.1 gather_fusion
  61.2 3.6 fusion.34
  65.6 2.1 gather_fusion
  69.0 3.6 fusion.34
  73.4 2.1 gather_fusion
  76.7 3.6 fusion.34
  81.1 2.1 gather_fusion
  84.4 3.6 fusion.34
  88.8 2.1 gather_fusion
  92.2 3.6 fusion.34
  96.6 2.1 gather_fusion
  99.9 3.6 fusion.34
  104.3 2.1 gather_fusion
  107.7 3.6 fusion.34
  115.4 3.6 fusion.34
  123.1 3.6 fusion.34
  129.6 118.4 %psum.7 = f32[64,64]{1,0:T(8,128)S(1)} all-reduce(f32[64,64]{1,0:T(8,128)S(1)} %fusion.20), channel_id=1, replica_groups=mesh['rows'=64,'sub'=8] {'rows','sub'}, use_global_device_ids=true, to_apply=%region_2.4 | all-reduce | flops 4096 | bytes 32768 | tf_op jit(solution)/shard_map/psum | solution.py:92
  248.0 97.8 %while.47 = (s32[]{:T(128)}, f32[64,64]{1,0:T(8,128)S(1)}, f32[64,64]{1,0:T(8,128)S(1)}, s32[]{:T(128)}, s32[]{:T(128)}) while((s32[]{:T(128)}, f32[64,64]{1,0:T(8,128)S(1)}, f32[64,64]{1,0:T(8,128)S(1)}, s32[]{:T(128)}, s32[]{:T(128)}) %tuple.112), condition=%wide.region_6.8_spmd.clone.clone, body=%wide.region_3.7_spmd.clone.clone.sunk | while | flops 29122 | bytes 84067 | solution.py:59
  345.8 101.2 %while.46 = (s32[]{:T(128)}, f32[64,64]{1,0:T(8,128)S(1)}, f32[64,64]{1,0:T(8,128)S(1)}, s32[]{:T(128)}, s32[]{:T(128)}, /*index=5*/s32[]{:T(128)}) while((s32[]{:T(128)}, f32[64,64]{1,0:T(8,128)S(1)}, f32[64,64]{1,0:T(8,128)S(1)}, s32[]{:T(128)}, s32[]{:T(128)}, /*index=5*/s32[]{:T(128)}) %tuple.115), condition=%wide.region_10.12_spmd.clone, body=%wide.region_7.11_spmd.clone.sunk | while | flops 74243 | bytes 67696 | solution.py:75
  (730 shorter events, 194.2 us)
Async XLA Ops:
  0.6 19.1 %collective-permute-start.2 = (s32[2,32]{1,0:T(2,128)}, s32[2,32]{1,0:T(2,128)S(1)}, u32[]{:S(2)}, u32[]{:S(2)}) collective-permute-start(s32[2,32]{1,0:T(2,128)} %param.17), channel_id=1, source_target_pairs={{0,1},{1,2},{2,3},{3,4},{4,5},{5,6},{6,7},{7,8},{8,9},{9,10},{10,1... | collective-permute-start | bytes 776 | tf_op jit(solution)/shard_map/ppermute | solution.py:19
  5.2 14.6 %collective-permute-start.3 = (s32[2,32]{1,0:T(2,128)}, s32[2,32]{1,0:T(2,128)S(1)}, u32[]{:S(2)}, u32[]{:S(2)}) collective-permute-start(s32[2,32]{1,0:T(2,128)} %param.17), channel_id=1, source_target_pairs={{1,0},{2,1},{3,2},{4,3},{5,4},{6,5},{7,6},{8,7},{9,8},{10,9},{11,1... | collective-permute-start | bytes 776 | tf_op jit(solution)/shard_map/ppermute | solution.py:21
  13.1 8.3 %collective-permute-start = (f32[8,64,128]{1,0,2:T(8,128)}, f32[8,64,128]{1,0,2:T(8,128)}, u32[]{:S(2)}, u32[]{:S(2)}) collective-permute-start(f32[8,64,128]{1,0,2:T(8,128)} %get-tuple-element.383), channel_id=1, source_target_pairs={{0,1},{1,2},{2,3},{3,4},{4,5},{5,6},{6,7},{7,8},{8,9},{9,10},{10,1... | collective-permute-start | bytes 786440 | tf_op jit(solution)/shard_map/ppermute | solution.py:19
  15.0 10.6 %collective-permute-start.1 = (f32[8,64,128]{1,0,2:T(8,128)S(1)}, f32[8,64,128]{1,0,2:T(8,128)}, u32[]{:S(2)}, u32[]{:S(2)}) collective-permute-start(f32[8,64,128]{1,0,2:T(8,128)S(1)} %get-tuple-element.384), channel_id=1, source_target_pairs={{1,0},{2,1},{3,2},{4,3},{5,4},{6,5},{7,6},{8,7},{9,8},{10,9},{11,1... | collective-permute-start | bytes 786440 | tf_op jit(solution)/shard_map/ppermute | solution.py:21
  28.3 5.7 %copy-start.1 = (s32[256]{0:T(256)S(1)}, s32[256]{0:T(256)}, u32[]{:S(2)}) copy-start(s32[256]{0:T(256)} %param.16) | copy-start | bytes 3076
  447.0 1.5 copy-start
where the time goes:
time: 452 us; the launch traced here: 449 us
  blocking collectives  118 us (26%)
  other arithmetic  114 us (25%)
  matrix products  97.2 us (22%)
  local copies, waits for them, and re-layouts  48.6 us (11%)
  loops' own time  48.3 us (11%)
  starting transfers between devices  15.2 us (3%)
  waiting for transfers between devices  5.74 us (1%)
    psum x1, blocking collectives, on_device(): total_gram = lax.psum(local_gram, ('rows', 'sub'))  118 us
    dot_general x64, matrix products, row_step(): partial_value = jnp.dot(upper_row, inverse, precision=lax.Precision.HIGHEST)  50.1 us
    another operation x1, loops' own time, cholesky_upper(): return lax.fori_loop(0, order, column_step, start)[1]  47.1 us
    dot_general x12, matrix products, add_slot(): jnp.einsum('ijb,jlb->ilb', coefficient, picked, precision=lax.Precision.H...  43.6 us
    reduce_sum x64, other arithmetic, row_step(): pivot = jnp.sum(upper_row * unit)  38.7 us
    reduce_sum x64, other arithmetic, column_step(): pivot = jnp.sqrt(jnp.sum(pivot_row * unit))  38.7 us
    gather x12, local copies, waits for them, and re-layouts, add_slot(): picked = jnp.take(extended, columns[slot_idx], axis=2)  24.9 us
    dynamic_slice x24, local copies, waits for them, and re-layouts, add_slot(): coefficient = values[slot_idx] * live_mask  15.1 us
  transfers between devices with their start and end apart: 4, of which 2 were waited for; matrix products, arithmetic and copies ran while one was open for 1% of the time, Pallas kernels for 0%

commit v1 on v0

v1 whole, which is shorter than its diff:
```python
import functools

import jax
import jax.numpy as jnp
from jax import lax
from jax.experimental import pallas as pl
from jax.experimental.pallas import tpu as pltpu
from jax.sharding import PartitionSpec as P

BLOCK = 8
LOADS = 64
SLOTS = 12
BROWS_DEV = 256
SEND = 32
CHIPS_X = 4
F32 = jnp.float32
BF16 = jnp.bfloat16
MESH = pl.DeviceIdType.MESH


def split3(value):
    high = value.astype(BF16)
    rest = value - high.astype(F32)
    mid = rest.astype(BF16)
    low = (rest - mid.astype(F32)).astype(BF16)
    return high, mid, low


def dot(a, b):
    return lax.dot_general(a, b, (((1,), (0,)), ((), ())), preferred_element_type=F32)


def one_hot(condition):
    return jnp.where(condition, 1.0, 0.0).astype(BF16)


def iota(shape, dim):
    return lax.broadcasted_iota(jnp.int32, shape, dim)


def factor_rows(M):
    M = list(M)
    outs = []
    full = (8, 128)
    for p in range(8):
        T = M[p]
        t = [jnp.broadcast_to(T[r : r + 1, :], full) for r in range(8)]
        s = {}
        for r in range(8):
            for m in range(r, 8):
                s[r, m] = jnp.broadcast_to(T[r : r + 1, 8 * p + m : 8 * p + m + 1], full)
        C = {}
        for q in range(p + 1, 8):
            for j in range(8):
                C[q, j] = jnp.broadcast_to(M[q][:, 8 * p + j : 8 * p + j + 1], full)
        inv, f, u = [], {}, []
        for j in range(8):
            r = lax.rsqrt(s[j, j])
            inv.append(r)
            for m in range(j + 1, 8):
                f[j, m] = s[j, m] * r
            u.append(t[j] * r)
            for m in range(j + 1, 8):
                for n in range(m, 8):
                    s[m, n] = s[m, n] - f[j, m] * f[j, n]
                t[m] = t[m] - f[j, m] * u[j]
        outs.append(u)
        if p == 7:
            break
        v = [None] * 8
        for j in range(7, -1, -1):
            a = u[j]
            for m in range(j + 1, 8):
                a = a - f[j, m] * v[m]
            v[j] = a * inv[j]
        for q in range(p + 1, 8):
            parts = [C[q, j] * v[j] for j in range(8)]
            while len(parts) > 1:
                parts = [parts[i] + parts[i + 1] for i in range(0, len(parts), 2)]
            M[q] = M[q] - parts[0]
    return outs


def kernel(nz, ny2, basis_ref, stiff_ref, cols_ref, count_ref, list_ref, out_ref, factor_ref,
           x_ref, s_ref, xt_ref, cc_ref, pick_ref, acc_ref, wt_ref, gst_ref,
           halo_out, halo_in, plane_out, plane_in, z_out, z_in, core_out, core_in, rows_ref,
           load_sem, halo_sem, plane_sem, z_sem, core_sem):
    nx = CHIPS_X
    rows = lax.axis_index("rows")
    sub = lax.axis_index("sub")
    z, x = rows // nx, rows % nx
    core = sub % 2
    slabs = nz * nx * ny2
    slab = rows * ny2 + sub
    nplane = nx * ny2
    me_plane = x * ny2 + sub

    def flat(index):
        return (index // ny2, index % ny2)

    prev_id, next_id = flat((slab + slabs - 1) % slabs), flat((slab + 1) % slabs)

    def plane_id(index):
        return (z * nx + index // ny2, index % ny2)

    def z_id(index):
        return (index * nx + x, sub)

    barrier = pltpu.get_barrier_semaphore()

    def greet(device):
        pl.semaphore_signal(barrier, inc=1, device_id=device, device_id_type=MESH)

    load_x = pltpu.make_async_copy(basis_ref, x_ref, load_sem.at[0])
    load_s = pltpu.make_async_copy(stiff_ref, s_ref, load_sem.at[1])
    load_x.start()
    load_s.start()
    greet(prev_id)
    greet(next_id)

    def greet_z(q, carry):
        greet(z_id((z + q) % nz))
        return carry

    def greet_plane(q, carry):
        greet(plane_id((me_plane + q) % nplane))
        return carry

    lax.fori_loop(1, nz, greet_z, 0)
    lax.fori_loop(1, nplane, greet_plane, 0)

    cols = cols_ref[...]
    live = iota(cols.shape, 0) < count_ref[...]
    from_prev = jnp.logical_and(cols >= BROWS_DEV, cols < BROWS_DEV + SEND)
    from_next = cols >= BROWS_DEV + SEND
    first = jnp.where(slab == 0, 1, 0)
    last = jnp.where(slab == slabs - 1, 1, 0)
    gone = jnp.where(from_prev, first, 0) + jnp.where(from_next, last, 0)
    cc_ref[...] = jnp.where(jnp.logical_and(live, gone == 0), cols, -1)

    load_x.wait()
    for j in range(BLOCK):
        for t, term in enumerate(split3(x_ref[j])):
            xt_ref[t, LOADS * j : LOADS * (j + 1), :] = term

    place = iota((BROWS_DEV, BROWS_DEV), 0)
    lane = iota((BROWS_DEV, BROWS_DEV), 1)
    lists = jnp.concatenate([list_ref[0:1, :]] * 4 + [list_ref[1:2, :]] * 4, axis=1)
    hit = place == lists
    packed = None
    for q in range(4):
        sel = one_hot(jnp.logical_and(hit, (lane % 128) // SEND == q))
        for t in range(3):
            term = dot(xt_ref[t, 128 * q : 128 * (q + 1), :], sel)
            packed = term if packed is None else packed + term
    halo_out[0] = packed[:, :128]
    halo_out[1] = packed[:, 128:]

    pl.semaphore_wait(barrier, 2 + (nz - 1) + (nplane - 1))
    to_prev = pltpu.make_async_remote_copy(
        src_ref=halo_out.at[0], dst_ref=halo_in.at[1], send_sem=halo_sem.at[0],
        recv_sem=halo_sem.at[1], device_id=prev_id, device_id_type=MESH)
    to_next = pltpu.make_async_remote_copy(
        src_ref=halo_out.at[1], dst_ref=halo_in.at[0], send_sem=halo_sem.at[2],
        recv_sem=halo_sem.at[3], device_id=next_id, device_id_type=MESH)
    to_prev.start()
    to_next.start()

    def pick_local(k, carry):
        sel = one_hot(place == cc_ref[pl.ds(k, 1), :])
        got = dot(xt_ref[0], sel) + dot(xt_ref[1], sel) + dot(xt_ref[2], sel)
        pick_ref[k] = got.reshape(BLOCK, LOADS, BROWS_DEV)
        return carry

    lax.fori_loop(1, SLOTS, pick_local, 0)
    load_s.wait()

    def multiply(k, source, start):
        for c in range(2):
            lanes = slice(128 * c, 128 * (c + 1))
            for h in range(2):
                loads = slice(32 * h, 32 * (h + 1))
                total = None if start else acc_ref[:, loads, lanes]
                for j in range(BLOCK):
                    term = s_ref[k, :, j : j + 1, lanes] * source(j, loads, lanes)[None]
                    total = term if total is None else total + term
                acc_ref[:, loads, lanes] = total

    multiply(0, lambda j, loads, lanes: x_ref[j, loads, lanes], True)

    to_prev.wait_recv()
    to_next.wait_recv()
    sides = [split3(halo_in[0]), split3(halo_in[1])]
    r = iota((BROWS_DEV, 192), 0)
    n = iota((BROWS_DEV, 192), 1)
    for q in range(4):
        total = None
        for t in range(3):
            want = (n % 64) // SEND * 128 + SEND * q + n % SEND
            sel = one_hot(jnp.logical_and(n // 64 == t, r == want))
            term = dot(sides[0][t], sel[:128]) + dot(sides[1][t], sel[128:])
            total = term if total is None else total + term
        gst_ref[128 * q : 128 * (q + 1), :] = total.astype(BF16)

    ghost_place = BROWS_DEV + iota((192, BROWS_DEV), 0) % 64

    def slot(k, carry):
        sel = one_hot(ghost_place == cc_ref[pl.ds(k, 1), :])
        got = dot(gst_ref[...], sel).reshape(BLOCK, LOADS, BROWS_DEV)
        pick_ref[k] = pick_ref[k] + got
        multiply(k, lambda j, loads, lanes: pick_ref[k, j, loads, lanes], False)
        return carry

    lax.fori_loop(1, SLOTS, slot, 0)

    gram = None
    for i in range(BLOCK):
        scaled = acc_ref[i] / s_ref[0, i, i : i + 1, :]
        wt_ref[i] = jnp.concatenate(split3(scaled), axis=0)
        term = lax.dot_general(wt_ref[i], wt_ref[i], (((1,), (1,)), ((), ())),
                               preferred_element_type=F32)
        gram = term if gram is None else gram + term
    gram = gram[0:64] + gram[64:128] + gram[128:192]
    gram = gram[:, 0:64] + gram[:, 64:128] + gram[:, 128:192]
    gram = gram * (1.0 / (BLOCK * BROWS_DEV * slabs))

    for c in range(2):
        plane_out[c] = jnp.concatenate([gram[32 * c : 32 * c + 16], gram[32 * c + 16 : 32 * c + 32]], axis=1)
    plane_in[me_plane] = plane_out[core]

    def send_plane(q, carry):
        to = (me_plane + q) % nplane
        pltpu.make_async_remote_copy(
            src_ref=plane_out.at[to % 2], dst_ref=plane_in.at[me_plane], send_sem=plane_sem.at[0],
            recv_sem=plane_sem.at[1], device_id=plane_id(to), device_id_type=MESH).start()
        return carry

    lax.fori_loop(1, nplane, send_plane, 0)
    part = plane_in.at[pl.ds(0, nplane - 1)]
    plane_all = pltpu.make_async_remote_copy(
        src_ref=part, dst_ref=part, send_sem=plane_sem.at[0], recv_sem=plane_sem.at[1],
        device_id=plane_id((me_plane + 1) % nplane), device_id_type=MESH)
    plane_all.wait_recv()
    total = jnp.sum(plane_in[...], axis=0)
    z_out[...] = total
    z_in[z] = total

    def send_z(q, carry):
        to = (z + q) % nz
        pltpu.make_async_remote_copy(
            src_ref=z_out, dst_ref=z_in.at[z], send_sem=z_sem.at[0],
            recv_sem=z_sem.at[1], device_id=z_id(to), device_id_type=MESH).start()
        return carry

    lax.fori_loop(1, nz, send_z, 0)
    part = z_in.at[pl.ds(0, nz - 1)]
    z_all = pltpu.make_async_remote_copy(
        src_ref=part, dst_ref=part, send_sem=z_sem.at[0], recv_sem=z_sem.at[1],
        device_id=z_id((z + 1) % nz), device_id_type=MESH)
    z_all.wait_recv()
    total = jnp.sum(z_in[...], axis=0)
    core_out[...] = total
    core_in[core] = total
    to_core = pltpu.make_async_remote_copy(
        src_ref=core_out, dst_ref=core_in.at[core], send_sem=core_sem.at[0],
        recv_sem=core_sem.at[1], device_id=(rows, sub + 1 - 2 * core), device_id_type=MESH)
    to_core.start()
    to_core.wait_recv()

    eye = jnp.where(iota((16, 64), 1) == iota((16, 64), 0), 1.0, 0.0)
    blocks = []
    for c in range(2):
        half = core_in[c]
        for g in range(2):
            base = 32 * c + 16 * g
            unit = jnp.where(iota((16, 64), 1) == iota((16, 64), 0) + base, 1.0, 0.0)
            both = jnp.concatenate([half[:, 64 * g : 64 * (g + 1)], unit], axis=1)
            blocks += [both[0:8], both[8:16]]
    outs = factor_rows(blocks)
    for p in range(8):
        for j in range(8):
            rows_ref[8 * p + j : 8 * p + j + 1, :] = outs[p][j][0:1]
    found = rows_ref[...]
    upper = iota((64, 64), 0) <= iota((64, 64), 1)
    factor_ref[...] = jnp.where(upper, found[:, :64], 0.0)
    left = jnp.concatenate([jnp.concatenate([term] * 3, axis=1) for term in split3(found[:, 64:])], axis=0)
    for i in range(BLOCK):
        got = dot(left, wt_ref[i])
        out_ref[i] = got[0:64] + got[64:128] + got[128:192]

    to_prev.wait_send()
    to_next.wait_send()
    plane_all.wait_send()
    z_all.wait_send()
    to_core.wait_send()


def on_device(nz, ny2, basis, stiffness, col_index, block_count, send_list):
    nplane = CHIPS_X * ny2
    vmem = pl.BlockSpec(memory_space=pltpu.VMEM)
    hbm = pl.BlockSpec(memory_space=pl.ANY)
    return pl.pallas_call(
        functools.partial(kernel, nz, ny2),
        out_shape=(jax.ShapeDtypeStruct(basis.shape, F32), jax.ShapeDtypeStruct((LOADS, LOADS), F32)),
        in_specs=[hbm, hbm, vmem, vmem, vmem],
        out_specs=(vmem, vmem),
        scratch_shapes=[
            pltpu.VMEM((BLOCK, LOADS, BROWS_DEV), F32),
            pltpu.VMEM((SLOTS, BLOCK, BLOCK, BROWS_DEV), F32),
            pltpu.VMEM((3, BLOCK * LOADS, BROWS_DEV), BF16),
            pltpu.VMEM((SLOTS, BROWS_DEV), jnp.int32),
            pltpu.VMEM((SLOTS, BLOCK, LOADS, BROWS_DEV), F32),
            pltpu.VMEM((BLOCK, LOADS, BROWS_DEV), F32),
            pltpu.VMEM((BLOCK, 3 * LOADS, BROWS_DEV), BF16),
            pltpu.VMEM((BLOCK * LOADS, 192), BF16),
            pltpu.VMEM((2, 128, 128), F32),
            pltpu.VMEM((2, 128, 128), F32),
            pltpu.VMEM((2, 16, 128), F32),
            pltpu.VMEM((nplane, 16, 128), F32),
            pltpu.VMEM((16, 128), F32),
            pltpu.VMEM((nz, 16, 128), F32),
            pltpu.VMEM((16, 128), F32),
            pltpu.VMEM((2, 16, 128), F32),
            pltpu.VMEM((LOADS, 128), F32),
            pltpu.SemaphoreType.DMA((2,)),
            pltpu.SemaphoreType.DMA((4,)),
            pltpu.SemaphoreType.DMA((2,)),
            pltpu.SemaphoreType.DMA((2,)),
            pltpu.SemaphoreType.DMA((2,)),
        ],
        name="arnoldi_step",
        compiler_params=pltpu.CompilerParams(
            collective_id=1, has_side_effects=True, vmem_limit_bytes=48 * 1024 * 1024),
    )(basis, stiffness, col_index, block_count.reshape(1, BROWS_DEV), send_list)


def solution(mesh):
    nz, ny2 = mesh.shape["rows"] // CHIPS_X, mesh.shape["sub"]
    in_specs = (
        P(None, None, ("rows", "sub")),
        P(None, None, None, ("rows", "sub")),
        P(None, ("rows", "sub")),
        P(("rows", "sub")),
        P(None, ("rows", "sub")),
    )
    out_specs = (P(None, None, ("rows", "sub")), P())
    return jax.shard_map(
        functools.partial(on_device, nz, ny2), mesh=mesh, in_specs=in_specs, out_specs=out_specs,
        check_vma=False,
    )
```

time: 452 us -> 54.9 us (0.12)
  blocking collectives: 118 us -> 0 us
  other arithmetic: 114 us -> 0 us
  matrix products: 97.2 us -> 0 us
  Pallas kernels: 0 us -> 48.3 us
  loops' own time: 48.3 us -> 0 us
  local copies, waits for them, and re-layouts: 48.6 us -> 5.65 us
  starting transfers between devices: 15.2 us -> 0 us
  waiting for transfers between devices: 5.74 us -> 0 us
    psum x1 -> x0, blocking collectives: 118 us -> none  [on_device(): total_gram = lax.psum(local_gram, ('rows', 'sub'))]
    dot_general x78 -> x0, matrix products: 97.2 us -> none  [the longest x64 50.1 us: row_step(): partial_value = jnp.dot(upper_row, inverse, precision=lax.Precision.HIGHEST)]
    reduce_sum x256 -> x0, other arithmetic: 89.5 us -> none  [the longest x64 38.7 us: row_step(): pivot = jnp.sum(upper_row * unit)]
    pallas_call x0 -> x1, Pallas kernels: none -> 48.3 us  [on_device(): pl.pallas_call(functools.partial(kernel, nz, ny2), out_shape=(jax.ShapeDt...]
    another operation x3 -> x0, loops' own time: 48.3 us -> none  [the longest x1 47.1 us: cholesky_upper(): return lax.fori_loop(0, order, column_step, start)[1]]
    gather x16 -> x0, local copies, waits for them, and re-layouts: 29.9 us -> none  [the longest x12 24.9 us: add_slot(): picked = jnp.take(extended, columns[slot_idx], axis=2)]
    ppermute x4 -> x0, starting transfers between devices: 15.2 us -> none  [the longest x2 8.68 us: padded_2(): lax.ppermute(head, axis, [((i + 1) % count, i) for i in range(ends)])]
    dynamic_slice x24 -> x0, local copies, waits for them, and re-layouts: 15.1 us -> none  [add_slot(): coefficient = values[slot_idx] * live_mask]
  transfers between devices with their start and end apart: 4 -> 0, of which waited for: 2 -> 0; matrix products, arithmetic and copies ran while one was open for 1% -> 0% of each run, Pallas kernels for 0% -> 0%
where the time goes in v1:
time: 54.9 us; the launch traced here: 54.7 us
  Pallas kernels  48.3 us (88%)
  local copies, waits for them, and re-layouts  5.65 us (10%)
  between operations  0.65 us (1%)
    pallas_call x1, Pallas kernels, on_device(): pl.pallas_call(functools.partial(kernel, nz, ny2), out_shape=(jax.ShapeDt...  48.3 us
    unnamed x12, local copies, waits for them, and re-layouts  5.65 us

profile of v1, /device:TPU:1, one launch (start us, length us, event | category | flops | bytes accessed | tf_op | source)
XLA Modules:
  0.0 54.7 jit_solution(2016192225978286364)
XLA Ops:
  0.6 0.0 copy-start.3
  0.6 0.7 %copy-done.3 = s32[256]{0:T(256)S(1)} copy-done((s32[256]{0:T(256)S(1)}, s32[256]{0:T(256)}, u32[]{:S(2)}) %copy-start.3) | copy-done | bytes 1048
  1.3 0.0 copy-start
  1.3 1.1 %copy-done = f32[12,8,8,256]{3,2,1,0:T(8,128)S(1)} copy-done((f32[12,8,8,256]{3,2,1,0:T(8,128)S(1)}, f32[12,8,8,256]{3,2,1,0:T(8,128)}, u32[]{:S(2)}) %copy-start) | copy-done | bytes 786456
  2.4 0.0 copy-start.1
  2.4 1.0 %copy-done.1 = f32[8,64,256]{2,1,0:T(8,128)S(1)} copy-done((f32[8,64,256]{2,1,0:T(8,128)S(1)}, f32[8,64,256]{2,1,0:T(8,128)}, u32[]{:S(2)}) %copy-start.1) | copy-done | bytes 524312
  3.5 0.0 copy-start.2
  3.5 0.7 %copy-done.2 = s32[12,256]{1,0:T(8,128)S(1)} copy-done((s32[12,256]{1,0:T(8,128)S(1)}, s32[12,256]{1,0:T(8,128)}, u32[]{:S(2)}) %copy-start.2) | copy-done | bytes 12312
  4.2 0.0 copy-start.4
  4.2 0.7 %copy-done.4 = s32[2,32]{1,0:T(2,128)S(1)} copy-done((s32[2,32]{1,0:T(2,128)S(1)}, s32[2,32]{1,0:T(2,128)}, u32[]{:S(2)}) %copy-start.4) | copy-done | bytes 280
  4.9 48.3 %arnoldi_step.1 = (f32[8,64,256]{2,1,0:T(8,128)S(1)}, f32[64,64]{1,0:T(8,128)S(1)}) custom-call(f32[8,64,256]{2,1,0:T(8,128)S(1)} %copy-done.1, f32[12,8,8,256]{3,2,1,0:T(8,128)S(1)} %copy-done, s32[12,256]{1,0:T(8,128)S(1)} %copy-done.2, s32[1,256]{1,0:T(1,128)S(1)} %bitcast.1, s32[2,32]{1,0:T(2,128)S(1)} %copy-done.4), custom_call_target="tpu_custom_call" | custom-call | tf_op jit(solution)/shard_map/arnoldi_step/pallas_call | solution.py:302
  53.2 0.8 %copy.9 = f32[8,64,256]{2,1,0:T(8,128)} copy(f32[8,64,256]{2,1,0:T(8,128)S(1)} %get-tuple-element.4) | data formatting | bytes 1048576
  54.0 0.6 %copy.10 = f32[64,64]{1,0:T(8,128)} copy(f32[64,64]{1,0:T(8,128)S(1)} %get-tuple-element.5) | data formatting | bytes 32768
Async XLA Ops:
  0.6 0.7 %copy-start.3 = (s32[256]{0:T(256)S(1)}, s32[256]{0:T(256)}, u32[]{:S(2)}) copy-start(s32[256]{0:T(256)} %param.8) | copy-start | bytes 3076
  1.3 1.1 %copy-start = (f32[12,8,8,256]{3,2,1,0:T(8,128)S(1)}, f32[12,8,8,256]{3,2,1,0:T(8,128)}, u32[]{:S(2)}) copy-start(f32[12,8,8,256]{3,2,1,0:T(8,128)} %stiff_ref.1) | copy-start | bytes 2359300
  2.4 1.0 %copy-start.1 = (f32[8,64,256]{2,1,0:T(8,128)S(1)}, f32[8,64,256]{2,1,0:T(8,128)}, u32[]{:S(2)}) copy-start(f32[8,64,256]{2,1,0:T(8,128)} %basis_ref.1) | copy-start | bytes 1572868
  3.5 0.7 %copy-start.2 = (s32[12,256]{1,0:T(8,128)S(1)}, s32[12,256]{1,0:T(8,128)}, u32[]{:S(2)}) copy-start(s32[12,256]{1,0:T(8,128)} %cols_ref.1) | copy-start | bytes 36868
  4.2 0.7 %copy-start.4 = (s32[2,32]{1,0:T(2,128)S(1)}, s32[2,32]{1,0:T(2,128)}, u32[]{:S(2)}) copy-start(s32[2,32]{1,0:T(2,128)} %list_ref.1) | copy-start | bytes 772

commit v2 on v1

--- a/solution.py
+++ b/solution.py
@@ -81,10 +81,10 @@
     return outs
 
 
-def kernel(nz, ny2, basis_ref, stiff_ref, cols_ref, count_ref, list_ref, out_ref, factor_ref,
-           x_ref, s_ref, xt_ref, cc_ref, pick_ref, acc_ref, wt_ref, gst_ref,
-           halo_out, halo_in, plane_out, plane_in, z_out, z_in, core_out, core_in, rows_ref,
-           load_sem, halo_sem, plane_sem, z_sem, core_sem):
+def kernel(nz, ny2, basis_ref, stiff_ref, cols_hbm, count_hbm, list_hbm, wt_ref, sum_ref,
+           x_ref, s_ref, cols_ref, count_ref, list_ref, xt_ref, cc_ref, pick_ref, acc_ref, gst_ref,
+           halo_out, halo_in, plane_out, plane_in, z_out, z_in, core_out,
+           load_sem, halo_sem, plane_sem, z_sem, core_sem, near_sem, far_sem):
     nx = CHIPS_X
     rows = lax.axis_index("rows")
     sub = lax.axis_index("sub")
@@ -100,9 +100,6 @@
 
     prev_id, next_id = flat((slab + slabs - 1) % slabs), flat((slab + 1) % slabs)
 
-    def plane_id(index):
-        return (z * nx + index // ny2, index % ny2)
-
     def z_id(index):
         return (index * nx + x, sub)
 
@@ -113,22 +110,26 @@
 
     load_x = pltpu.make_async_copy(basis_ref, x_ref, load_sem.at[0])
     load_s = pltpu.make_async_copy(stiff_ref, s_ref, load_sem.at[1])
+    load_c = pltpu.make_async_copy(cols_hbm, cols_ref, load_sem.at[2])
+    load_n = pltpu.make_async_copy(count_hbm, count_ref, load_sem.at[3])
+    load_l = pltpu.make_async_copy(list_hbm, list_ref, load_sem.at[4])
+    load_l.start()
     load_x.start()
+    load_c.start()
+    load_n.start()
     load_s.start()
     greet(prev_id)
     greet(next_id)
-
-    def greet_z(q, carry):
-        greet(z_id((z + q) % nz))
-        return carry
-
-    def greet_plane(q, carry):
-        greet(plane_id((me_plane + q) % nplane))
-        return carry
-
-    lax.fori_loop(1, nz, greet_z, 0)
-    lax.fori_loop(1, nplane, greet_plane, 0)
-
+    for q in range(1, ny2):
+        greet((rows, (sub + q) % ny2))
+    x_peers = [(z * nx + (x + q) % nx, sub) for q in range(1, nx)]
+    for peer in x_peers:
+        greet(peer)
+    greet(z_id((z + 1) % nz))
+    greet(z_id((z + nz - 1) % nz))
+
+    load_c.wait()
+    load_n.wait()
     cols = cols_ref[...]
     live = iota(cols.shape, 0) < count_ref[...]
     from_prev = jnp.logical_and(cols >= BROWS_DEV, cols < BROWS_DEV + SEND)
@@ -138,6 +139,7 @@
     gone = jnp.where(from_prev, first, 0) + jnp.where(from_next, last, 0)
     cc_ref[...] = jnp.where(jnp.logical_and(live, gone == 0), cols, -1)
 
+    load_l.wait()
     load_x.wait()
     for j in range(BLOCK):
         for t, term in enumerate(split3(x_ref[j])):
@@ -156,7 +158,7 @@
     halo_out[0] = packed[:, :128]
     halo_out[1] = packed[:, 128:]
 
-    pl.semaphore_wait(barrier, 2 + (nz - 1) + (nplane - 1))
+    pl.semaphore_wait(barrier, 2 + (ny2 - 1) + (nx - 1) + 2)
     to_prev = pltpu.make_async_remote_copy(
         src_ref=halo_out.at[0], dst_ref=halo_in.at[1], send_sem=halo_sem.at[0],
         recv_sem=halo_sem.at[1], device_id=prev_id, device_id_type=MESH)
@@ -165,6 +167,19 @@
         recv_sem=halo_sem.at[3], device_id=next_id, device_id_type=MESH)
     to_prev.start()
     to_next.start()
+    for peer in x_peers:
+        pl.semaphore_signal(near_sem, inc=1, device_id=peer, device_id_type=MESH)
+
+    def tell(step):
+        for to in ((z + step) % nz, (z + nz - step) % nz):
+            pl.semaphore_signal(far_sem.at[step.bit_length() - 1], inc=1, device_id=z_id(to), device_id_type=MESH)
+
+    def hear(step):
+        pl.semaphore_wait(far_sem.at[step.bit_length() - 1], 2)
+
+    steps = [1 << e for e in range(8) if 2 * (1 << e) <= nz // 2]
+    if steps:
+        tell(steps[0])
 
     def pick_local(k, carry):
         sel = one_hot(place == cc_ref[pl.ds(k, 1), :])
@@ -190,6 +205,9 @@
 
     to_prev.wait_recv()
     to_next.wait_recv()
+    if len(steps) > 1:
+        hear(steps[0])
+        tell(steps[1])
     sides = [split3(halo_in[0]), split3(halo_in[1])]
     r = iota((BROWS_DEV, 192), 0)
     n = iota((BROWS_DEV, 192), 1)
@@ -204,14 +222,24 @@
 
     ghost_place = BROWS_DEV + iota((192, BROWS_DEV), 0) % 64
 
-    def slot(k, carry):
+    def add_ghosts(k, carry):
         sel = one_hot(ghost_place == cc_ref[pl.ds(k, 1), :])
         got = dot(gst_ref[...], sel).reshape(BLOCK, LOADS, BROWS_DEV)
         pick_ref[k] = pick_ref[k] + got
-        multiply(k, lambda j, loads, lanes: pick_ref[k, j, loads, lanes], False)
         return carry
 
-    lax.fori_loop(1, SLOTS, slot, 0)
+    lax.fori_loop(1, SLOTS, add_ghosts, 0)
+    for c in range(2):
+        lanes = slice(128 * c, 128 * (c + 1))
+        for h in range(2):
+            loads = slice(32 * h, 32 * (h + 1))
+
+            def slot(k, total):
+                for j in range(BLOCK):
+                    total = total + s_ref[k, :, j : j + 1, lanes] * pick_ref[k, j, loads, lanes][None]
+                return total
+
+            acc_ref[:, loads, lanes] = lax.fori_loop(1, SLOTS, slot, acc_ref[:, loads, lanes])
 
     gram = None
     for i in range(BLOCK):
@@ -224,35 +252,44 @@
     gram = gram[:, 0:64] + gram[:, 64:128] + gram[:, 128:192]
     gram = gram * (1.0 / (BLOCK * BROWS_DEV * slabs))
 
-    for c in range(2):
-        plane_out[c] = jnp.concatenate([gram[32 * c : 32 * c + 16], gram[32 * c + 16 : 32 * c + 32]], axis=1)
+    pack(plane_out, gram)
+    pl.semaphore_wait(near_sem, nx - 1)
     plane_in[me_plane] = plane_out[core]
 
-    def send_plane(q, carry):
-        to = (me_plane + q) % nplane
-        pltpu.make_async_remote_copy(
-            src_ref=plane_out.at[to % 2], dst_ref=plane_in.at[me_plane], send_sem=plane_sem.at[0],
-            recv_sem=plane_sem.at[1], device_id=plane_id(to), device_id_type=MESH).start()
-        return carry
-
-    lax.fori_loop(1, nplane, send_plane, 0)
+    for dx in (2, 1, 3, 0):
+        for dy in range(ny2):
+            shift = (ny2 // 2 + dy) % ny2
+            if dx or shift:
+                to_x, to_sub = (x + dx) % nx, (sub + shift) % ny2
+                pltpu.make_async_remote_copy(
+                    src_ref=plane_out.at[to_sub % 2], dst_ref=plane_in.at[me_plane],
+                    send_sem=plane_sem.at[0], recv_sem=plane_sem.at[1],
+                    device_id=(z * nx + to_x, to_sub), device_id_type=MESH).start()
+
+    for e in range(1, len(steps) - 1):
+        hear(steps[e])
+        tell(steps[e + 1])
     part = plane_in.at[pl.ds(0, nplane - 1)]
     plane_all = pltpu.make_async_remote_copy(
         src_ref=part, dst_ref=part, send_sem=plane_sem.at[0], recv_sem=plane_sem.at[1],
-        device_id=plane_id((me_plane + 1) % nplane), device_id_type=MESH)
+        device_id=(rows, sub + 1 - 2 * core), device_id_type=MESH)
     plane_all.wait_recv()
     total = jnp.sum(plane_in[...], axis=0)
     z_out[...] = total
     z_in[z] = total
 
+    if steps:
+        hear(steps[-1])
+
     def send_z(q, carry):
-        to = (z + q) % nz
+        half = (q + 1) // 2
+        to = (z + nz // 2 + half * (1 - 2 * (q % 2))) % nz
         pltpu.make_async_remote_copy(
             src_ref=z_out, dst_ref=z_in.at[z], send_sem=z_sem.at[0],
             recv_sem=z_sem.at[1], device_id=z_id(to), device_id_type=MESH).start()
         return carry
 
-    lax.fori_loop(1, nz, send_z, 0)
+    lax.fori_loop(0, nz - 1, send_z, 0)
     part = z_in.at[pl.ds(0, nz - 1)]
     z_all = pltpu.make_async_remote_copy(
         src_ref=part, dst_ref=part, send_sem=z_sem.at[0], recv_sem=z_sem.at[1],
@@ -260,33 +297,12 @@
     z_all.wait_recv()
     total = jnp.sum(z_in[...], axis=0)
     core_out[...] = total
-    core_in[core] = total
+    sum_ref[core] = total
     to_core = pltpu.make_async_remote_copy(
-        src_ref=core_out, dst_ref=core_in.at[core], send_sem=core_sem.at[0],
+        src_ref=core_out, dst_ref=sum_ref.at[core], send_sem=core_sem.at[0],
         recv_sem=core_sem.at[1], device_id=(rows, sub + 1 - 2 * core), device_id_type=MESH)
     to_core.start()
     to_core.wait_recv()
-
-    eye = jnp.where(iota((16, 64), 1) == iota((16, 64), 0), 1.0, 0.0)
-    blocks = []
-    for c in range(2):
-        half = core_in[c]
-        for g in range(2):
-            base = 32 * c + 16 * g
-            unit = jnp.where(iota((16, 64), 1) == iota((16, 64), 0) + base, 1.0, 0.0)
-            both = jnp.concatenate([half[:, 64 * g : 64 * (g + 1)], unit], axis=1)
-            blocks += [both[0:8], both[8:16]]
-    outs = factor_rows(blocks)
-    for p in range(8):
-        for j in range(8):
-            rows_ref[8 * p + j : 8 * p + j + 1, :] = outs[p][j][0:1]
-    found = rows_ref[...]
-    upper = iota((64, 64), 0) <= iota((64, 64), 1)
-    factor_ref[...] = jnp.where(upper, found[:, :64], 0.0)
-    left = jnp.concatenate([jnp.concatenate([term] * 3, axis=1) for term in split3(found[:, 64:])], axis=0)
-    for i in range(BLOCK):
-        got = dot(left, wt_ref[i])
-        out_ref[i] = got[0:64] + got[64:128] + got[128:192]
 
     to_prev.wait_send()
     to_next.wait_send()
@@ -295,43 +311,114 @@
     to_core.wait_send()
 
 
+def pack(ref, gram):
+    wide = [gram[0:16], jnp.concatenate([gram[16:32, 16:64], gram[32:48, 32:48]], axis=1)]
+    small = [gram[48:64, 48:64], gram[32:48, 48:64]]
+    for c in range(2):
+        ref[c, 0:8, :] = jnp.concatenate([wide[c][0:8], wide[c][8:16]], axis=1)
+        ref[c, 8:10, :] = jnp.concatenate([small[c][2 * i : 2 * i + 2] for i in range(8)], axis=1)
+
+
+def unpack(ref):
+    wide = [jnp.concatenate([ref[c, 0:8, 0:64], ref[c, 0:8, 64:128]], axis=0) for c in range(2)]
+    small = [jnp.concatenate([ref[c, 8:10, 16 * i : 16 * (i + 1)] for i in range(8)], axis=0) for c in range(2)]
+    zeros = jnp.zeros((16, 48), F32)
+    rows = [
+        wide[0],
+        jnp.concatenate([zeros[:, 0:16], wide[1][:, 0:48]], axis=1),
+        jnp.concatenate([zeros[:, 0:32], wide[1][:, 48:64], small[1]], axis=1),
+        jnp.concatenate([zeros, small[0]], axis=1),
+    ]
+    upper = jnp.concatenate(rows, axis=0)
+    keep = iota((LOADS, LOADS), 0) <= iota((LOADS, LOADS), 1)
+    return jnp.where(keep, upper, upper.T)
+
+
+def apply_kernel(wt_ref, sum_ref, out_hbm, factor_hbm, out_ref, factor_ref, rows_ref, sems):
+    gram = unpack(sum_ref)
+    unit = jnp.where(iota((LOADS, LOADS), 0) == iota((LOADS, LOADS), 1), 1.0, 0.0)
+    both = jnp.concatenate([gram, unit], axis=1)
+    outs = factor_rows([both[8 * p : 8 * p + 8] for p in range(8)])
+    for p in range(8):
+        for j in range(8):
+            rows_ref[8 * p + j : 8 * p + j + 1, :] = outs[p][j][0:1]
+    found = rows_ref[...]
+    upper = iota((LOADS, LOADS), 0) <= iota((LOADS, LOADS), 1)
+    factor_ref[...] = jnp.where(upper, found[:, :LOADS], 0.0)
+    store = pltpu.make_async_copy(factor_ref, factor_hbm, sems.at[BLOCK])
+    store.start()
+    stores = [store]
+    left = jnp.concatenate([jnp.concatenate([term] * 3, axis=1) for term in split3(found[:, LOADS:])], axis=0)
+    for i in range(BLOCK):
+        got = dot(left, wt_ref[i])
+        out_ref[i] = got[0:64] + got[64:128] + got[128:192]
+        store = pltpu.make_async_copy(out_ref.at[i], out_hbm.at[i], sems.at[i])
+        store.start()
+        stores.append(store)
+    for store in stores:
+        store.wait()
+
+
 def on_device(nz, ny2, basis, stiffness, col_index, block_count, send_list):
     nplane = CHIPS_X * ny2
     vmem = pl.BlockSpec(memory_space=pltpu.VMEM)
-    hbm = pl.BlockSpec(memory_space=pl.ANY)
-    return pl.pallas_call(
+    hbm = pl.BlockSpec(memory_space=pltpu.MemorySpace.HBM)
+    held = [
+        pltpu.with_memory_space_constraint(value, pltpu.MemorySpace.HBM)
+        for value in (basis, stiffness, col_index, block_count.reshape(1, BROWS_DEV), send_list)
+    ]
+    wt, total = pl.pallas_call(
         functools.partial(kernel, nz, ny2),
-        out_shape=(jax.ShapeDtypeStruct(basis.shape, F32), jax.ShapeDtypeStruct((LOADS, LOADS), F32)),
-        in_specs=[hbm, hbm, vmem, vmem, vmem],
+        out_shape=(
+            jax.ShapeDtypeStruct((BLOCK, 3 * LOADS, BROWS_DEV), BF16),
+            jax.ShapeDtypeStruct((2, 10, 128), F32),
+        ),
+        in_specs=[hbm, hbm, hbm, hbm, hbm],
         out_specs=(vmem, vmem),
         scratch_shapes=[
             pltpu.VMEM((BLOCK, LOADS, BROWS_DEV), F32),
             pltpu.VMEM((SLOTS, BLOCK, BLOCK, BROWS_DEV), F32),
+            pltpu.VMEM((SLOTS, BROWS_DEV), jnp.int32),
+            pltpu.VMEM((1, BROWS_DEV), jnp.int32),
+            pltpu.VMEM((2, SEND), jnp.int32),
             pltpu.VMEM((3, BLOCK * LOADS, BROWS_DEV), BF16),
             pltpu.VMEM((SLOTS, BROWS_DEV), jnp.int32),
             pltpu.VMEM((SLOTS, BLOCK, LOADS, BROWS_DEV), F32),
             pltpu.VMEM((BLOCK, LOADS, BROWS_DEV), F32),
-            pltpu.VMEM((BLOCK, 3 * LOADS, BROWS_DEV), BF16),
             pltpu.VMEM((BLOCK * LOADS, 192), BF16),
             pltpu.VMEM((2, 128, 128), F32),
             pltpu.VMEM((2, 128, 128), F32),
-            pltpu.VMEM((2, 16, 128), F32),
-            pltpu.VMEM((nplane, 16, 128), F32),
-            pltpu.VMEM((16, 128), F32),
-            pltpu.VMEM((nz, 16, 128), F32),
-            pltpu.VMEM((16, 128), F32),
-            pltpu.VMEM((2, 16, 128), F32),
-            pltpu.VMEM((LOADS, 128), F32),
-            pltpu.SemaphoreType.DMA((2,)),
+            pltpu.VMEM((2, 10, 128), F32),
+            pltpu.VMEM((nplane, 10, 128), F32),
+            pltpu.VMEM((10, 128), F32),
+            pltpu.VMEM((nz, 10, 128), F32),
+            pltpu.VMEM((10, 128), F32),
+            pltpu.SemaphoreType.DMA((5,)),
             pltpu.SemaphoreType.DMA((4,)),
             pltpu.SemaphoreType.DMA((2,)),
             pltpu.SemaphoreType.DMA((2,)),
             pltpu.SemaphoreType.DMA((2,)),
+            pltpu.SemaphoreType.REGULAR,
+            pltpu.SemaphoreType.REGULAR((4,)),
         ],
         name="arnoldi_step",
         compiler_params=pltpu.CompilerParams(
-            collective_id=1, has_side_effects=True, vmem_limit_bytes=48 * 1024 * 1024),
-    )(basis, stiffness, col_index, block_count.reshape(1, BROWS_DEV), send_list)
+            collective_id=1, has_side_effects=True, vmem_limit_bytes=40 * 1024 * 1024),
+    )(*held)
+    return pl.pallas_call(
+        apply_kernel,
+        out_shape=(jax.ShapeDtypeStruct(basis.shape, F32), jax.ShapeDtypeStruct((LOADS, LOADS), F32)),
+        in_specs=[vmem, vmem],
+        out_specs=(hbm, hbm),
+        scratch_shapes=[
+            pltpu.VMEM((BLOCK, LOADS, BROWS_DEV), F32),
+            pltpu.VMEM((LOADS, LOADS), F32),
+            pltpu.VMEM((LOADS, 128), F32),
+            pltpu.SemaphoreType.DMA((BLOCK + 1,)),
+        ],
+        name="apply",
+        compiler_params=pltpu.CompilerParams(vmem_limit_bytes=16 * 1024 * 1024),
+    )(wt, total)
 
 
 def solution(mesh):

time: 54.9 us -> 46.2 us (0.84)
  local copies, waits for them, and re-layouts: 5.65 us -> 0 us
  Pallas kernels: 48.3 us -> 45.4 us
    pallas_call x1, Pallas kernels: 48.3 us -> 41.5 us  [on_device(): pl.pallas_call(functools.partial(kernel, nz, ny2), out_shape=(jax.ShapeDt...]
    unnamed x12 -> x0, local copies, waits for them, and re-layouts: 5.65 us -> none
    pallas_call x0 -> x1, Pallas kernels: none -> 3.95 us  [on_device(): pl.pallas_call(apply_kernel, out_shape=(jax.ShapeDtypeStruct(basis.shape,...]
where the time goes in v2:
time: 46.2 us; the launch traced here: 46.1 us
  Pallas kernels  45.4 us (98%)
  between operations  0.64 us (1%)
    pallas_call x1, Pallas kernels, on_device(): pl.pallas_call(functools.partial(kernel, nz, ny2), out_shape=(jax.ShapeDt...  41.5 us
    pallas_call x1, Pallas kernels, on_device(): pl.pallas_call(apply_kernel, out_shape=(jax.ShapeDtypeStruct(basis.shape,...  3.95 us

profile of v2, /device:TPU:1, one launch (start us, length us, event | category | flops | bytes accessed | tf_op | source)
XLA Modules:
  0.0 46.1 jit_solution(2732888896942410911)
XLA Ops:
  0.6 41.5 %arnoldi_step.1 = (bf16[8,192,256]{2,1,0:T(8,128)(2,1)S(1)}, f32[2,10,128]{2,1,0:T(8,128)S(1)}) custom-call(f32[8,64,256]{2,1,0:T(8,128)} %basis_ref.1, f32[12,8,8,256]{3,2,1,0:T(8,128)} %stiff_ref.1, s32[12,256]{1,0:T(8,128)} %cols_hbm.1, s32[1,256]{1,0:T(1,128)} %bitcast.1, s32[2,32]{1,0:T(2,128)} %list_hbm.1), custom_call_target="tpu_custom_call" | custom-call | tf_op jit(solution)/shard_map/arnoldi_step/pallas_call | solution.py:370
  42.1 4.0 %apply.1 = (f32[8,64,256]{2,1,0:T(8,128)}, f32[64,64]{1,0:T(8,128)}) custom-call(bf16[8,192,256]{2,1,0:T(8,128)(2,1)S(1)} %get-tuple-element.4.wt_ref, f32[2,10,128]{2,1,0:T(8,128)S(1)} %get-tuple-element.5.sum_ref), custom_call_target="tpu_custom_call" | custom-call | tf_op jit(solution)/shard_map/apply/pallas_call | solution.py:408

commit v3 on v2

--- a/solution.py
+++ b/solution.py
@@ -38,21 +38,24 @@
     return lax.broadcasted_iota(jnp.int32, shape, dim)
 
 
-def factor_rows(M):
+def factor_rows(M, cols_ref):
     M = list(M)
     outs = []
     full = (8, 128)
     for p in range(8):
         T = M[p]
-        t = [jnp.broadcast_to(T[r : r + 1, :], full) for r in range(8)]
+        cols_ref[p, 8] = T
+        C = {}
+        for q in range(p, 8):
+            for j in range(8):
+                C[q, j] = jnp.broadcast_to(M[q][:, 8 * p + j : 8 * p + j + 1], full)
+        for j in range(8):
+            cols_ref[p, j] = C[p, j]
+        t = [jnp.broadcast_to(cols_ref[p, 8, r : r + 1, :], full) for r in range(8)]
         s = {}
         for r in range(8):
             for m in range(r, 8):
-                s[r, m] = jnp.broadcast_to(T[r : r + 1, 8 * p + m : 8 * p + m + 1], full)
-        C = {}
-        for q in range(p + 1, 8):
-            for j in range(8):
-                C[q, j] = jnp.broadcast_to(M[q][:, 8 * p + j : 8 * p + j + 1], full)
+                s[r, m] = jnp.broadcast_to(cols_ref[p, m, r : r + 1, :], full)
         inv, f, u = [], {}, []
         for j in range(8):
             r = lax.rsqrt(s[j, j])
@@ -82,7 +85,7 @@
 
 
 def kernel(nz, ny2, basis_ref, stiff_ref, cols_hbm, count_hbm, list_hbm, wt_ref, sum_ref,
-           x_ref, s_ref, cols_ref, count_ref, list_ref, xt_ref, cc_ref, pick_ref, acc_ref, gst_ref,
+           x_ref, s_ref, cols_ref, count_ref, list_ref, xt_ref, cc_ref, pick_ref, acc_ref, gst_ref, sel_ref,
            halo_out, halo_in, plane_out, plane_in, z_out, z_in, core_out,
            load_sem, halo_sem, plane_sem, z_sem, core_sem, near_sem, far_sem):
     nx = CHIPS_X
@@ -189,6 +192,9 @@
 
     lax.fori_loop(1, SLOTS, pick_local, 0)
     load_s.wait()
+    if len(steps) > 1:
+        hear(steps[0])
+        tell(steps[1])
 
     def multiply(k, source, start):
         for c in range(2):
@@ -203,36 +209,38 @@
 
     multiply(0, lambda j, loads, lanes: x_ref[j, loads, lanes], True)
 
-    to_prev.wait_recv()
-    to_next.wait_recv()
-    if len(steps) > 1:
-        hear(steps[0])
-        tell(steps[1])
-    sides = [split3(halo_in[0]), split3(halo_in[1])]
     r = iota((BROWS_DEV, 192), 0)
     n = iota((BROWS_DEV, 192), 1)
     for q in range(4):
+        want = (n % 64) // SEND * 128 + SEND * q + n % SEND
+        for t in range(3):
+            sel_ref[q, t] = one_hot(jnp.logical_and(n // 64 == t, r == want))
+
+    to_prev.wait_recv()
+    to_next.wait_recv()
+    sides = [split3(halo_in[0]), split3(halo_in[1])]
+    for q in range(4):
         total = None
         for t in range(3):
-            want = (n % 64) // SEND * 128 + SEND * q + n % SEND
-            sel = one_hot(jnp.logical_and(n // 64 == t, r == want))
-            term = dot(sides[0][t], sel[:128]) + dot(sides[1][t], sel[128:])
+            term = dot(sides[0][t], sel_ref[q, t, :128]) + dot(sides[1][t], sel_ref[q, t, 128:])
             total = term if total is None else total + term
         gst_ref[128 * q : 128 * (q + 1), :] = total.astype(BF16)
 
     ghost_place = BROWS_DEV + iota((192, BROWS_DEV), 0) % 64
 
     def add_ghosts(k, carry):
-        sel = one_hot(ghost_place == cc_ref[pl.ds(k, 1), :])
+        sel = one_hot(ghost_place == cc_ref[k : k + 1, :])
         got = dot(gst_ref[...], sel).reshape(BLOCK, LOADS, BROWS_DEV)
         pick_ref[k] = pick_ref[k] + got
         return carry
 
-    lax.fori_loop(1, SLOTS, add_ghosts, 0)
+    for k in range(1, SLOTS):
+        add_ghosts(k, 0)
     for c in range(2):
         lanes = slice(128 * c, 128 * (c + 1))
-        for h in range(2):
-            loads = slice(32 * h, 32 * (h + 1))
+
+        for h in range(LOADS // 16):
+            loads = slice(16 * h, 16 * (h + 1))
 
             def slot(k, total):
                 for j in range(BLOCK):
@@ -240,6 +248,9 @@
                 return total
 
             acc_ref[:, loads, lanes] = lax.fori_loop(1, SLOTS, slot, acc_ref[:, loads, lanes])
+        if c == 0 and len(steps) > 2:
+            hear(steps[1])
+            tell(steps[2])
 
     gram = None
     for i in range(BLOCK):
@@ -266,9 +277,6 @@
                     send_sem=plane_sem.at[0], recv_sem=plane_sem.at[1],
                     device_id=(z * nx + to_x, to_sub), device_id_type=MESH).start()
 
-    for e in range(1, len(steps) - 1):
-        hear(steps[e])
-        tell(steps[e + 1])
     part = plane_in.at[pl.ds(0, nplane - 1)]
     plane_all = pltpu.make_async_remote_copy(
         src_ref=part, dst_ref=part, send_sem=plane_sem.at[0], recv_sem=plane_sem.at[1],
@@ -334,11 +342,11 @@
     return jnp.where(keep, upper, upper.T)
 
 
-def apply_kernel(wt_ref, sum_ref, out_hbm, factor_hbm, out_ref, factor_ref, rows_ref, sems):
+def apply_kernel(wt_ref, sum_ref, out_hbm, factor_hbm, out_ref, factor_ref, rows_ref, cols_ref, sems):
     gram = unpack(sum_ref)
     unit = jnp.where(iota((LOADS, LOADS), 0) == iota((LOADS, LOADS), 1), 1.0, 0.0)
     both = jnp.concatenate([gram, unit], axis=1)
-    outs = factor_rows([both[8 * p : 8 * p + 8] for p in range(8)])
+    outs = factor_rows([both[8 * p : 8 * p + 8] for p in range(8)], cols_ref)
     for p in range(8):
         for j in range(8):
             rows_ref[8 * p + j : 8 * p + j + 1, :] = outs[p][j][0:1]
@@ -386,6 +394,7 @@
             pltpu.VMEM((SLOTS, BLOCK, LOADS, BROWS_DEV), F32),
             pltpu.VMEM((BLOCK, LOADS, BROWS_DEV), F32),
             pltpu.VMEM((BLOCK * LOADS, 192), BF16),
+            pltpu.VMEM((4, 3, BROWS_DEV, 192), BF16),
             pltpu.VMEM((2, 128, 128), F32),
             pltpu.VMEM((2, 128, 128), F32),
             pltpu.VMEM((2, 10, 128), F32),
@@ -414,6 +423,7 @@
             pltpu.VMEM((BLOCK, LOADS, BROWS_DEV), F32),
             pltpu.VMEM((LOADS, LOADS), F32),
             pltpu.VMEM((LOADS, 128), F32),
+            pltpu.VMEM((8, 9, 8, 128), F32),
             pltpu.SemaphoreType.DMA((BLOCK + 1,)),
         ],
         name="apply",

time: 46.2 us -> 44.3 us (0.959)
  Pallas kernels: 45.4 us -> 43.6 us
    pallas_call x1, Pallas kernels: 41.5 us -> 39.8 us  [on_device(): pl.pallas_call(functools.partial(kernel, nz, ny2), out_shape=(jax.ShapeDt...]
where the time goes in v3:
time: 44.3 us; the launch traced here: 44.2 us
  Pallas kernels  43.6 us (98%)
  between operations  0.64 us (1%)
    pallas_call x1, Pallas kernels, on_device(): pl.pallas_call(functools.partial(kernel, nz, ny2), out_shape=(jax.ShapeDt...  39.8 us
    pallas_call x1, Pallas kernels, on_device(): pl.pallas_call(apply_kernel, out_shape=(jax.ShapeDtypeStruct(basis.shape,...  3.75 us

profile of v3, /device:TPU:1, one launch (start us, length us, event | category | flops | bytes accessed | tf_op | source)
XLA Modules:
  0.0 44.2 jit_solution(9397042223620720048)
XLA Ops:
  0.6 39.8 %arnoldi_step.1 = (bf16[8,192,256]{2,1,0:T(8,128)(2,1)S(1)}, f32[2,10,128]{2,1,0:T(8,128)S(1)}) custom-call(f32[8,64,256]{2,1,0:T(8,128)} %basis_ref.1, f32[12,8,8,256]{3,2,1,0:T(8,128)} %stiff_ref.1, s32[12,256]{1,0:T(8,128)} %cols_hbm.1, s32[1,256]{1,0:T(1,128)} %bitcast.1, s32[2,32]{1,0:T(2,128)} %list_hbm.1), custom_call_target="tpu_custom_call" | custom-call | tf_op jit(solution)/shard_map/arnoldi_step/pallas_call | solution.py:378
  40.5 3.7 %apply.1 = (f32[8,64,256]{2,1,0:T(8,128)}, f32[64,64]{1,0:T(8,128)}) custom-call(bf16[8,192,256]{2,1,0:T(8,128)(2,1)S(1)} %get-tuple-element.4.wt_ref, f32[2,10,128]{2,1,0:T(8,128)S(1)} %get-tuple-element.5.sum_ref), custom_call_target="tpu_custom_call" | custom-call | tf_op jit(solution)/shard_map/apply/pallas_call | solution.py:417

commit v4 on v3

--- a/solution.py
+++ b/solution.py
@@ -38,7 +38,7 @@
     return lax.broadcasted_iota(jnp.int32, shape, dim)
 
 
-def factor_rows(M, cols_ref):
+def factor_rows(M, cols_ref, near_ref):
     M = list(M)
     outs = []
     full = (8, 128)
@@ -46,37 +46,58 @@
         T = M[p]
         cols_ref[p, 8] = T
         C = {}
-        for q in range(p, 8):
+        for q in range(p + 1, 8):
             for j in range(8):
                 C[q, j] = jnp.broadcast_to(M[q][:, 8 * p + j : 8 * p + j + 1], full)
+        if p == 0:
+            corner = [jnp.broadcast_to(T[:, j : j + 1], full) for j in range(8)]
         for j in range(8):
-            cols_ref[p, j] = C[p, j]
+            cols_ref[p, j] = corner[j]
+        if p < 7:
+            corner = [jnp.broadcast_to(M[p + 1][:, 8 * p + 8 + j : 8 * p + 9 + j], full) for j in range(8)]
         t = [jnp.broadcast_to(cols_ref[p, 8, r : r + 1, :], full) for r in range(8)]
         s = {}
         for r in range(8):
             for m in range(r, 8):
                 s[r, m] = jnp.broadcast_to(cols_ref[p, m, r : r + 1, :], full)
-        inv, f, u = [], {}, []
-        for j in range(8):
-            r = lax.rsqrt(s[j, j])
-            inv.append(r)
-            for m in range(j + 1, 8):
-                f[j, m] = s[j, m] * r
-            u.append(t[j] * r)
-            for m in range(j + 1, 8):
+        inv, f, u = [None] * 8, {}, [None] * 8
+        near = [C[p + 1, j] for j in range(8)] if p < 7 else None
+        for j in range(0, 8, 2):
+            a, b = s[j, j], s[j, j + 1]
+            first = lax.rsqrt(a)
+            both = lax.rsqrt(a * s[j + 1, j + 1] - b * b)
+            second = first * both
+            inv[j], inv[j + 1] = first, a * first * both
+            f[j, j + 1] = b * first
+            for m in range(j + 2, 8):
+                f[j, m] = s[j, m] * first
+                f[j + 1, m] = (a * s[j + 1, m] - b * s[j, m]) * second
+            u[j], u[j + 1] = t[j] * first, (a * t[j + 1] - b * t[j]) * second
+            for m in range(j + 2, 8):
                 for n in range(m, 8):
-                    s[m, n] = s[m, n] - f[j, m] * f[j, n]
-                t[m] = t[m] - f[j, m] * u[j]
+                    s[m, n] = s[m, n] - f[j, m] * f[j, n] - f[j + 1, m] * f[j + 1, n]
+                t[m] = t[m] - f[j, m] * u[j] - f[j + 1, m] * u[j + 1]
+            if near:
+                e0, e1 = near[j] * first, (a * near[j + 1] - b * near[j]) * second
+                for m in range(j + 2, 8):
+                    near[m] = near[m] - f[j, m] * e0 - f[j + 1, m] * e1
+                M[p + 1] = M[p + 1] - e0 * u[j] - e1 * u[j + 1]
+                near_ref[p, j] = e0
+                near_ref[p, j + 1] = e1
+                for m in range(8):
+                    d0 = jnp.broadcast_to(near_ref[p, j, m : m + 1, :], full)
+                    d1 = jnp.broadcast_to(near_ref[p, j + 1, m : m + 1, :], full)
+                    corner[m] = corner[m] - e0 * d0 - e1 * d1
         outs.append(u)
-        if p == 7:
-            break
+        if p >= 6:
+            continue
         v = [None] * 8
         for j in range(7, -1, -1):
             a = u[j]
             for m in range(j + 1, 8):
                 a = a - f[j, m] * v[m]
             v[j] = a * inv[j]
-        for q in range(p + 1, 8):
+        for q in range(p + 2, 8):
             parts = [C[q, j] * v[j] for j in range(8)]
             while len(parts) > 1:
                 parts = [parts[i] + parts[i + 1] for i in range(0, len(parts), 2)]
@@ -85,7 +106,7 @@
 
 
 def kernel(nz, ny2, basis_ref, stiff_ref, cols_hbm, count_hbm, list_hbm, wt_ref, sum_ref,
-           x_ref, s_ref, cols_ref, count_ref, list_ref, xt_ref, cc_ref, pick_ref, acc_ref, gst_ref, sel_ref,
+           x_ref, s_ref, cols_ref, count_ref, list_ref, xt_ref, cc_ref, pick_ref, acc_ref, gst_ref, sel_ref, ghost_ref,
            halo_out, halo_in, plane_out, plane_in, z_out, z_in, core_out,
            load_sem, halo_sem, plane_sem, z_sem, core_sem, near_sem, far_sem):
     nx = CHIPS_X
@@ -216,6 +237,8 @@
         for t in range(3):
             sel_ref[q, t] = one_hot(jnp.logical_and(n // 64 == t, r == want))
 
+    ghost_place = BROWS_DEV + iota((192, BROWS_DEV), 0) % 64
+
     to_prev.wait_recv()
     to_next.wait_recv()
     sides = [split3(halo_in[0]), split3(halo_in[1])]
@@ -225,8 +248,6 @@
             term = dot(sides[0][t], sel_ref[q, t, :128]) + dot(sides[1][t], sel_ref[q, t, 128:])
             total = term if total is None else total + term
         gst_ref[128 * q : 128 * (q + 1), :] = total.astype(BF16)
-
-    ghost_place = BROWS_DEV + iota((192, BROWS_DEV), 0) % 64
 
     def add_ghosts(k, carry):
         sel = one_hot(ghost_place == cc_ref[k : k + 1, :])
@@ -342,17 +363,21 @@
     return jnp.where(keep, upper, upper.T)
 
 
-def apply_kernel(wt_ref, sum_ref, out_hbm, factor_hbm, out_ref, factor_ref, rows_ref, cols_ref, sems):
+def apply_kernel(wt_ref, sum_ref, out_hbm, factor_hbm, out_ref, factor_ref, rows_ref, cols_ref, near_ref, sems):
     gram = unpack(sum_ref)
-    unit = jnp.where(iota((LOADS, LOADS), 0) == iota((LOADS, LOADS), 1), 1.0, 0.0)
-    both = jnp.concatenate([gram, unit], axis=1)
-    outs = factor_rows([both[8 * p : 8 * p + 8] for p in range(8)], cols_ref)
+    on_diagonal = iota((LOADS, LOADS), 0) == iota((LOADS, LOADS), 1)
+    diagonal = jnp.where(on_diagonal, gram, 0.0)
+    square = jnp.sum(diagonal, axis=0, keepdims=True)
+    lane_scale = lax.rsqrt(square)
+    row_scale = lax.rsqrt(jnp.sum(diagonal, axis=1, keepdims=True))
+    both = jnp.concatenate([gram * row_scale * lane_scale, jnp.where(on_diagonal, lane_scale, 0.0)], axis=1)
+    outs = factor_rows([both[8 * p : 8 * p + 8] for p in range(8)], cols_ref, near_ref)
     for p in range(8):
         for j in range(8):
             rows_ref[8 * p + j : 8 * p + j + 1, :] = outs[p][j][0:1]
     found = rows_ref[...]
     upper = iota((LOADS, LOADS), 0) <= iota((LOADS, LOADS), 1)
-    factor_ref[...] = jnp.where(upper, found[:, :LOADS], 0.0)
+    factor_ref[...] = jnp.where(upper, found[:, :LOADS] * (square * lane_scale), 0.0)
     store = pltpu.make_async_copy(factor_ref, factor_hbm, sems.at[BLOCK])
     store.start()
     stores = [store]
@@ -395,6 +420,7 @@
             pltpu.VMEM((BLOCK, LOADS, BROWS_DEV), F32),
             pltpu.VMEM((BLOCK * LOADS, 192), BF16),
             pltpu.VMEM((4, 3, BROWS_DEV, 192), BF16),
+            pltpu.VMEM((SLOTS, 192, BROWS_DEV), BF16),
             pltpu.VMEM((2, 128, 128), F32),
             pltpu.VMEM((2, 128, 128), F32),
             pltpu.VMEM((2, 10, 128), F32),
@@ -424,6 +450,7 @@
             pltpu.VMEM((LOADS, LOADS), F32),
             pltpu.VMEM((LOADS, 128), F32),
             pltpu.VMEM((8, 9, 8, 128), F32),
+            pltpu.VMEM((8, 8, 8, 128), F32),
             pltpu.SemaphoreType.DMA((BLOCK + 1,)),
         ],
         name="apply",

time: 44.3 us -> 43.3 us (0.977)
  Pallas kernels: 43.6 us -> 42.5 us
    pallas_call x1, Pallas kernels: 3.75 us -> 2.66 us  [on_device(): pl.pallas_call(apply_kernel, out_shape=(jax.ShapeDtypeStruct(basis.shape,...]
where the time goes in v4:
time: 43.3 us; the launch traced here: 43.1 us
  Pallas kernels  42.5 us (98%)
  between operations  0.64 us (1%)
    pallas_call x1, Pallas kernels, on_device(): pl.pallas_call(functools.partial(kernel, nz, ny2), out_shape=(jax.ShapeDt...  39.8 us
    pallas_call x1, Pallas kernels, on_device(): pl.pallas_call(apply_kernel, out_shape=(jax.ShapeDtypeStruct(basis.shape,...  2.66 us

profile of v4, /device:TPU:1, one launch (start us, length us, event | category | flops | bytes accessed | tf_op | source)
XLA Modules:
  0.0 43.1 jit_solution(13132435973074730313)
XLA Ops:
  0.6 39.8 %arnoldi_step.1 = (bf16[8,192,256]{2,1,0:T(8,128)(2,1)S(1)}, f32[2,10,128]{2,1,0:T(8,128)S(1)}) custom-call(f32[8,64,256]{2,1,0:T(8,128)} %basis_ref.1, f32[12,8,8,256]{3,2,1,0:T(8,128)} %stiff_ref.1, s32[12,256]{1,0:T(8,128)} %cols_hbm.1, s32[1,256]{1,0:T(1,128)} %bitcast.1, s32[2,32]{1,0:T(2,128)} %list_hbm.1), custom_call_target="tpu_custom_call" | custom-call | tf_op jit(solution)/shard_map/arnoldi_step/pallas_call | solution.py:403
  40.4 2.7 %apply.1 = (f32[8,64,256]{2,1,0:T(8,128)}, f32[64,64]{1,0:T(8,128)}) custom-call(bf16[8,192,256]{2,1,0:T(8,128)(2,1)S(1)} %get-tuple-element.4.wt_ref, f32[2,10,128]{2,1,0:T(8,128)S(1)} %get-tuple-element.5.sum_ref), custom_call_target="tpu_custom_call" | custom-call | tf_op jit(solution)/shard_map/apply/pallas_call | solution.py:443

commit v5 on v4

--- a/solution.py
+++ b/solution.py
@@ -107,8 +107,8 @@
 
 def kernel(nz, ny2, basis_ref, stiff_ref, cols_hbm, count_hbm, list_hbm, wt_ref, sum_ref,
            x_ref, s_ref, cols_ref, count_ref, list_ref, xt_ref, cc_ref, pick_ref, acc_ref, gst_ref, sel_ref, ghost_ref,
-           halo_out, halo_in, plane_out, plane_in, z_out, z_in, core_out,
-           load_sem, halo_sem, plane_sem, z_sem, core_sem, near_sem, far_sem):
+           halo_out, halo_in, plane_out, plane_in, z_out, z_in, core_out, direct_in,
+           load_sem, halo_sem, plane_sem, z_sem, core_sem, near_sem, far_sem, direct_sem):
     nx = CHIPS_X
     rows = lax.axis_index("rows")
     sub = lax.axis_index("sub")
@@ -152,6 +152,17 @@
     greet(z_id((z + 1) % nz))
     greet(z_id((z + nz - 1) % nz))
 
+    is_first = jnp.logical_and(rows == 0, sub == 1)
+
+    @pl.when(is_first)
+    def _():
+        greet((nx, 0))
+        greet(((nz - 1) * nx, 0))
+
+    is_source = jnp.logical_and(x == 0, sub == 0)
+    extra = jnp.where(jnp.logical_and(is_source, z == 1), 1, 0)
+    extra = extra + jnp.where(jnp.logical_and(is_source, z == nz - 1), 1, 0)
+
     load_c.wait()
     load_n.wait()
     cols = cols_ref[...]
@@ -182,7 +193,7 @@
     halo_out[0] = packed[:, :128]
     halo_out[1] = packed[:, 128:]
 
-    pl.semaphore_wait(barrier, 2 + (ny2 - 1) + (nx - 1) + 2)
+    pl.semaphore_wait(barrier, 2 + (ny2 - 1) + (nx - 1) + 2 + extra)
     to_prev = pltpu.make_async_remote_copy(
         src_ref=halo_out.at[0], dst_ref=halo_in.at[1], send_sem=halo_sem.at[0],
         recv_sem=halo_sem.at[1], device_id=prev_id, device_id_type=MESH)
@@ -309,6 +320,15 @@
 
     if steps:
         hear(steps[-1])
+
+    is_mate = jnp.logical_and(rows == 0, sub == 0)
+    direct = pltpu.make_async_remote_copy(
+        src_ref=z_out, dst_ref=direct_in.at[z], send_sem=direct_sem.at[0], recv_sem=direct_sem.at[1],
+        device_id=(0, 1), device_id_type=MESH)
+
+    @pl.when(is_source)
+    def _():
+        direct.start()
 
     def send_z(q, carry):
         half = (q + 1) // 2
@@ -330,14 +350,35 @@
     to_core = pltpu.make_async_remote_copy(
         src_ref=core_out, dst_ref=sum_ref.at[core], send_sem=core_sem.at[0],
         recv_sem=core_sem.at[1], device_id=(rows, sub + 1 - 2 * core), device_id_type=MESH)
-    to_core.start()
-    to_core.wait_recv()
+
+    @pl.when(jnp.logical_not(is_mate))
+    def _():
+        to_core.start()
+
+    @pl.when(jnp.logical_not(is_first))
+    def _():
+        to_core.wait_recv()
+
+    @pl.when(is_first)
+    def _():
+        pltpu.make_async_remote_copy(
+            src_ref=direct_in, dst_ref=direct_in, send_sem=direct_sem.at[0], recv_sem=direct_sem.at[1],
+            device_id=(0, 0), device_id_type=MESH).wait_recv()
+        sum_ref[0] = jnp.sum(direct_in[...], axis=0)
+
 
     to_prev.wait_send()
     to_next.wait_send()
     plane_all.wait_send()
     z_all.wait_send()
-    to_core.wait_send()
+
+    @pl.when(is_source)
+    def _():
+        direct.wait_send()
+
+    @pl.when(jnp.logical_not(is_mate))
+    def _():
+        to_core.wait_send()
 
 
 def pack(ref, gram):
@@ -428,6 +469,7 @@
             pltpu.VMEM((10, 128), F32),
             pltpu.VMEM((nz, 10, 128), F32),
             pltpu.VMEM((10, 128), F32),
+            pltpu.VMEM((nz, 10, 128), F32),
             pltpu.SemaphoreType.DMA((5,)),
             pltpu.SemaphoreType.DMA((4,)),
             pltpu.SemaphoreType.DMA((2,)),
@@ -435,6 +477,7 @@
             pltpu.SemaphoreType.DMA((2,)),
             pltpu.SemaphoreType.REGULAR,
             pltpu.SemaphoreType.REGULAR((4,)),
+            pltpu.SemaphoreType.DMA((2,)),
         ],
         name="arnoldi_step",
         compiler_params=pltpu.CompilerParams(

time: 43.3 us -> 42.3 us (0.977)
  Pallas kernels: 42.5 us -> 41.5 us
    pallas_call x1, Pallas kernels: 39.8 us -> 38.9 us  [on_device(): pl.pallas_call(functools.partial(kernel, nz, ny2), out_shape=(jax.ShapeDt...]
where the time goes in v5:
time: 42.3 us; the launch traced here: 42.2 us
  Pallas kernels  41.5 us (98%)
  between operations  0.64 us (2%)
    pallas_call x1, Pallas kernels, on_device(): pl.pallas_call(functools.partial(kernel, nz, ny2), out_shape=(jax.ShapeDt...  38.9 us
    pallas_call x1, Pallas kernels, on_device(): pl.pallas_call(apply_kernel, out_shape=(jax.ShapeDtypeStruct(basis.shape,...  2.67 us

profile of v5, /device:TPU:1, one launch (start us, length us, event | category | flops | bytes accessed | tf_op | source)
XLA Modules:
  0.0 42.2 jit_solution(175786964504260211)
XLA Ops:
  0.6 38.9 %arnoldi_step.1 = (bf16[8,192,256]{2,1,0:T(8,128)(2,1)S(1)}, f32[2,10,128]{2,1,0:T(8,128)S(1)}) custom-call(f32[8,64,256]{2,1,0:T(8,128)} %basis_ref.1, f32[12,8,8,256]{3,2,1,0:T(8,128)} %stiff_ref.1, s32[12,256]{1,0:T(8,128)} %cols_hbm.1, s32[1,256]{1,0:T(1,128)} %bitcast.1, s32[2,32]{1,0:T(2,128)} %list_hbm.1), custom_call_target="tpu_custom_call" | custom-call | tf_op jit(solution)/shard_map/arnoldi_step/pallas_call | solution.py:444
  39.5 2.7 %apply.1 = (f32[8,64,256]{2,1,0:T(8,128)}, f32[64,64]{1,0:T(8,128)}) custom-call(bf16[8,192,256]{2,1,0:T(8,128)(2,1)S(1)} %get-tuple-element.4.wt_ref, f32[2,10,128]{2,1,0:T(8,128)S(1)} %get-tuple-element.5.sum_ref), custom_call_target="tpu_custom_call" | custom-call | tf_op jit(solution)/shard_map/apply/pallas_call | solution.py:486

commit v6 on v5

--- a/solution.py
+++ b/solution.py
@@ -299,15 +299,22 @@
     pl.semaphore_wait(near_sem, nx - 1)
     plane_in[me_plane] = plane_out[core]
 
+    def send_plane(to_x, to_sub, wanted):
+        @pl.when(wanted)
+        def _():
+            pltpu.make_async_remote_copy(
+                src_ref=plane_out.at[to_sub % 2], dst_ref=plane_in.at[me_plane],
+                send_sem=plane_sem.at[0], recv_sem=plane_sem.at[1],
+                device_id=(z * nx + to_x, to_sub), device_id_type=MESH).start()
+
+    for to_sub in (0, 1):
+        send_plane(0, to_sub, me_plane != to_sub)
     for dx in (2, 1, 3, 0):
         for dy in range(ny2):
             shift = (ny2 // 2 + dy) % ny2
             if dx or shift:
                 to_x, to_sub = (x + dx) % nx, (sub + shift) % ny2
-                pltpu.make_async_remote_copy(
-                    src_ref=plane_out.at[to_sub % 2], dst_ref=plane_in.at[me_plane],
-                    send_sem=plane_sem.at[0], recv_sem=plane_sem.at[1],
-                    device_id=(z * nx + to_x, to_sub), device_id_type=MESH).start()
+                send_plane(to_x, to_sub, to_x * ny2 + to_sub >= 2)
 
     part = plane_in.at[pl.ds(0, nplane - 1)]
     plane_all = pltpu.make_async_remote_copy(

time: 42.3 us -> 42.1 us (level)
  no operation moved by 1% of the time
where the time goes in v6:
time: 42.1 us; the launch traced here: 41.9 us
  Pallas kernels  41.3 us (98%)
  between operations  0.64 us (2%)
    pallas_call x1, Pallas kernels, on_device(): pl.pallas_call(functools.partial(kernel, nz, ny2), out_shape=(jax.ShapeDt...  38.6 us
    pallas_call x1, Pallas kernels, on_device(): pl.pallas_call(apply_kernel, out_shape=(jax.ShapeDtypeStruct(basis.shape,...  2.68 us

profile of v6, /device:TPU:1, one launch (start us, length us, event | category | flops | bytes accessed | tf_op | source)
XLA Modules:
  0.0 41.9 jit_solution(623942392687685431)
XLA Ops:
  0.6 38.6 %arnoldi_step.1 = (bf16[8,192,256]{2,1,0:T(8,128)(2,1)S(1)}, f32[2,10,128]{2,1,0:T(8,128)S(1)}) custom-call(f32[8,64,256]{2,1,0:T(8,128)} %basis_ref.1, f32[12,8,8,256]{3,2,1,0:T(8,128)} %stiff_ref.1, s32[12,256]{1,0:T(8,128)} %cols_hbm.1, s32[1,256]{1,0:T(1,128)} %bitcast.1, s32[2,32]{1,0:T(2,128)} %list_hbm.1), custom_call_target="tpu_custom_call" | custom-call | tf_op jit(solution)/shard_map/arnoldi_step/pallas_call | solution.py:451
  39.2 2.7 %apply.1 = (f32[8,64,256]{2,1,0:T(8,128)}, f32[64,64]{1,0:T(8,128)}) custom-call(bf16[8,192,256]{2,1,0:T(8,128)(2,1)S(1)} %get-tuple-element.4.wt_ref, f32[2,10,128]{2,1,0:T(8,128)S(1)} %get-tuple-element.5.sum_ref), custom_call_target="tpu_custom_call" | custom-call | tf_op jit(solution)/shard_map/apply/pallas_call | solution.py:493
